TPU v7x, 32 devices: a whole 2x2x4 slice. The times are simulated.
32 devices in a mesh: ctx: 8 (over z, y), tp: 4 (over x, core).
Axes of the slice: x: 2, y: 2, z: 4, core: 2. Of those that a mesh axis runs over, the one named last changes fastest.
Arguments:
- tokens: bfloat16 [4096, 6144], P(('ctx', 'tp')), may hold values from -18 to 18
- w_query: bfloat16 [6144, 3072], P(None, 'tp'), may hold values from -1 to 1
- key_matrix: bfloat16 [6144, 512], P(None, 'tp'), may hold values from -1 to 1
- value_matrix: bfloat16 [6144, 512], P(None, 'tp'), may hold values from -0.078125 to 0.078125
- w_out: bfloat16 [3072, 6144], P('tp'), may hold values from -0.109375 to 0.109375
- span_order: int32 [8, 2], replicated, may hold values from 0 to 15, as said below
Outputs:
- attended: bfloat16 [4096, 6144], P(('ctx', 'tp'))
Inputs may be any that keep to these rules, and one draw needn't show every extreme that they name: `span_order`: row r is (p, 15 - p) with p a permutation of 0 to 7, so every span appears once.
All inputs are finite; a program needn't handle non-finite values.
Results may differ from a plain program's by a relative error of at most 0.014.
The roundings to bfloat16 on the way count: a program that leaves them out, or rounds other values in their place, can miss the bound.
Values may be sent and summed in bfloat16 or wider, within the bound.
A program may use at most 128 MiB of HBM per device.

v0:
```python
import math

import jax
import jax.numpy as jnp
from jax import lax
from jax.sharding import PartitionSpec as P

ROPE_BASE = 1000000.0


def rotary_embed(values, token_positions):
    half = values.shape[-1] // 2
    freq = ROPE_BASE ** (-(jnp.arange(half, dtype=jnp.float32) * 2.0) / values.shape[-1])
    angle = token_positions[:, None] * freq[None, :]
    cosine = jnp.cos(angle)[:, None, :]
    sine = jnp.sin(angle)[:, None, :]
    first = values[..., :half]
    second = values[..., half:]
    return jnp.concatenate(
        [first * cosine - second * sine, second * cosine + first * sine], axis=-1
    )


def body(tokens, w_query, key_matrix, value_matrix, w_out, span_order):
    rank = lax.axis_index("ctx")
    head_dim = key_matrix.shape[1]
    qcols = w_query.shape[1]
    group = qcols // head_dim
    inv_scale = 1.0 / math.sqrt(head_dim)
    piece = lax.all_gather(tokens, "tp", axis=0, tiled=True)
    projected = jnp.concatenate(
        [
            jnp.dot(piece, w_query, preferred_element_type=jnp.float32),
            jnp.dot(piece, key_matrix, preferred_element_type=jnp.float32),
            jnp.dot(piece, value_matrix, preferred_element_type=jnp.float32),
        ],
        axis=1,
    )
    block_rows = projected.shape[0]
    span = block_rows // 2
    flat = span_order.reshape(-1)
    mine = lax.dynamic_slice(span_order, (rank, jnp.int32(0)), (1, 2)).reshape(2)
    own_pos = (
        (mine[:, None] * span + jnp.arange(span, dtype=jnp.int32)[None, :])
        .reshape(-1)
        .astype(jnp.float32)
    )
    query_rows = rotary_embed(
        projected[:, :qcols].reshape(block_rows, group, head_dim), own_pos
    ).astype(jnp.bfloat16)
    key = (
        rotary_embed(
            projected[:, qcols : qcols + head_dim].reshape(block_rows, 1, head_dim), own_pos
        )
        .reshape(block_rows, head_dim)
        .astype(jnp.bfloat16)
    )
    value_rows = projected[:, qcols + head_dim :].astype(jnp.bfloat16)
    query_rows = (
        query_rows.reshape(2, span, group, head_dim)
        .transpose(0, 2, 1, 3)
        .reshape(2, group * span, head_dim)
    )
    query_pos = jnp.tile(own_pos.reshape(2, 1, span), (1, group, 1)).reshape(2, group * span)

    def update(state, query_c, pos_c, key_tile, value_tile, key_pos):
        top_old, total_old, accum_old = state
        score = (
            lax.dot_general(
                query_c, key_tile, (((1,), (1,)), ((), ())), preferred_element_type=jnp.float32
            )
            * inv_scale
        )
        keep = key_pos[None, :] <= pos_c[:, None]
        score = jnp.where(keep, score, -1e30)
        top_new = jnp.maximum(top_old, jnp.max(score, axis=1))
        weight = jnp.where(keep, jnp.exp(score - top_new[:, None]), 0.0)
        factor = jnp.exp(top_old - top_new)
        total_new = factor * total_old + jnp.sum(weight, axis=1)
        accum_new = factor[:, None] * accum_old + jnp.dot(
            weight.astype(jnp.bfloat16), value_tile, preferred_element_type=jnp.float32
        )
        return (top_new, total_new, accum_new)

    rows_q = group * span
    start_top = jnp.full((rows_q,), -1e30, jnp.float32)
    start_total = jnp.zeros((rows_q,), jnp.float32)
    start_accum = jnp.zeros((rows_q, head_dim), jnp.float32)
    initial = (start_top, start_total, start_accum, start_top, start_total, start_accum)
    key_piece = lax.all_gather(key, "ctx", axis=0, tiled=True)
    value_piece = lax.all_gather(value_rows, "ctx", axis=0, tiled=True)
    count = key_piece.shape[0]
    global_rows = jnp.arange(count, dtype=jnp.int32)
    which = (global_rows // span)[:, None] == jnp.arange(flat.shape[0], dtype=jnp.int32)[None, :]
    span_ids = jnp.sum(jnp.where(which, flat[None, :], 0), axis=1)
    key_positions = (span_ids * span + global_rows % span).astype(jnp.float32)
    tile = math.gcd(count, span)

    def one_tile(step, state):
        key_tile = lax.dynamic_slice_in_dim(key_piece, step * tile, tile, 0)
        value_tile = lax.dynamic_slice_in_dim(value_piece, step * tile, tile, 0)
        pos_tile = lax.dynamic_slice_in_dim(key_positions, step * tile, tile, 0)
        updated = []
        for half_index in range(2):
            part_state = state[3 * half_index : 3 * half_index + 3]
            query_c = query_rows[half_index]
            pos_c = query_pos[half_index]
            needed = jnp.min(pos_tile) <= jnp.max(pos_c)
            part_state = lax.cond(
                needed,
                lambda inner: update(inner, query_c, pos_c, key_tile, value_tile, pos_tile),
                lambda inner: inner,
                part_state,
            )
            updated.extend(part_state)
        return tuple(updated)

    folded = lax.fori_loop(0, count // tile, one_tile, initial)
    halves = []
    for half_index in range(2):
        total = folded[3 * half_index + 1]
        accum = folded[3 * half_index + 2]
        mixed = (accum / total[:, None]).astype(jnp.bfloat16)
        halves.append(
            mixed.reshape(group, span, head_dim).transpose(1, 0, 2).reshape(span, group * head_dim)
        )
    heads_out = jnp.concatenate(halves, axis=0)
    return lax.psum_scatter(
        jnp.dot(heads_out, w_out, preferred_element_type=jnp.float32).astype(jnp.bfloat16),
        "tp",
        scatter_dimension=0,
        tiled=True,
    )


def solution(mesh):
    return jax.shard_map(
        body,
        mesh=mesh,
        in_specs=(
            P(("ctx", "tp"), None),
            P(None, "tp"),
            P(None, "tp"),
            P(None, "tp"),
            P("tp", None),
            P(),
        ),
        out_specs=P(("ctx", "tp"), None),
        check_vma=False,
    )
```

profile of v0, /device:TPU:0, one launch (start us, length us, event | category | flops | bytes accessed | tf_op | source)
XLA Modules:
  0.0 354.1 jit_solution(6930187349816770406)
XLA Ops:
  7.6 50.4 %all-gather.5.cloned.1.call-done = bf16[512,6144]{1,0:T(8,128)(2,1)} async-done(((bf16[128,6144]{1,0:T(8,128)(2,1)}), bf16[512,6144]{1,0:T(8,128)(2,1)}) %all-gather.5.cloned.1.call-update) | async-done | bytes 6291472 | tf_op jit(solution)/shard_map/all_gather | solution.py:30
  58.0 5.0 %convolution_bitcast_fusion = f32[512,1,128]{0,2,1:T(8,128)S(1)} fusion(bf16[512,6144]{1,0:T(8,128)(2,1)} %all-gather.5.cloned.1.call-done, bf16[6144,128]{1,0:T(8,128)(2,1)S(1)} %copy-done), kind=kOutput, calls=%fused_computation.37 | convolution fusion | flops 805306368 | bytes 8126464 | tf_op jit(solution)/shard_map/dot_general | solution.py:34
  66.4 5.6 %convolution_convert_fusion.1 = bf16[512,128]{1,0:T(8,128)(2,1)} fusion(bf16[512,6144]{1,0:T(8,128)(2,1)} %all-gather.5.cloned.1.call-done, bf16[6144,128]{1,0:T(8,128)(2,1)} %param.15), kind=kOutput, calls=%fused_computation.38 | convolution fusion | flops 805371904 | bytes 7995392 | tf_op jit(solution)/shard_map/dot_general | solution.py:35
  72.3 9.6 %fusion.50 = f32[512,768]{0,1:T(8,128)S(1)} fusion(bf16[512,6144]{1,0:T(8,128)(2,1)} %all-gather.5.cloned.1.call-done, bf16[6144,768]{1,0:T(8,128)(2,1)} %param.13), kind=kOutput, calls=%fused_computation.86 | convolution fusion | flops 4831838208 | bytes 17301504 | tf_op jit(solution)/shard_map/dot_general | solution.py:33
  83.4 1.8 copy.23
  85.2 18.8 %all-gather.9.cloned.1.call-done = bf16[4096,1,128]{0,2,1:T(8,128)(2,1)} async-done(((bf16[512,1,128]{0,2,1:T(8,128)(2,1)}), bf16[4096,1,128]{0,2,1:T(8,128)(2,1)}) %all-gather.9.cloned.1.call-update) | async-done | bytes 1048592 | tf_op jit(solution)/shard_map/all_gather | solution.py:90
  104.0 41.2 %all-gather.7.cloned.1.call-done = bf16[4096,128]{1,0:T(8,128)(2,1)} async-done(((bf16[512,128]{1,0:T(8,128)(2,1)}), bf16[4096,128]{1,0:T(8,128)(2,1)}) %all-gather.7.cloned.1.call-update) | async-done | bytes 1048592 | tf_op jit(solution)/shard_map/all_gather | solution.py:91
  145.3 133.1 %while.25 = (s32[]{:T(128)}, f32[1536]{0:T(1024)S(1)}, f32[1536]{0:T(1024)S(1)}, f32[1536,128]{1,0:T(8,128)S(1)}, f32[1536]{0:T(1024)S(1)}, /*index=5*/f32[1536]...) while((s32[]{:T(128)}, f32[1536]{0:T(1024)S(1)}, ...), condition=%wide.region_13.14_spmd.clone, body=%wide.region_3.13_spmd.clone.sunk | while | flops 412883200 | bytes 14330351 | solution.py:118
  149.7 2.6 conditional.7
  149.8 1.4 fusion.48
  153.5 2.6 conditional.6
  160.5 2.6 conditional.7
  160.6 1.4 fusion.48
  168.7 2.6 conditional.7
  172.4 2.6 conditional.6
  185.0 2.6 conditional.7
  185.0 1.4 fusion.48
  188.7 2.6 conditional.6
  201.3 2.6 conditional.7
  205.1 2.6 conditional.6
  217.6 2.6 conditional.7
  217.7 1.4 fusion.48
  221.4 2.6 conditional.6
  233.9 2.6 conditional.7
  237.7 2.6 conditional.6
  250.2 2.6 conditional.7
  250.3 1.4 fusion.48
  254.0 2.6 conditional.6
  266.5 2.6 conditional.7
  270.3 2.6 conditional.6
  279.4 10.8 %convolution_convert_fusion = bf16[512,6144]{1,0:T(8,128)(2,1)} fusion(bf16[768,6144]{1,0:T(8,128)(2,1)} %param.16, bf16[256,768]{0,1:T(8,128)(2,1)S(1)} %bitcast.61, bf16[256,768]{0,1:T(8,128)(2,1)S(1)} %bitcast.60), kind=kOutput, calls=%fused_computation.36 | convolution fusion | flops 4836556800 | bytes 16515072 | tf_op jit(solution)/shard_map/dot_general | solution.py:129
  290.3 57.3 %reduce-scatter.2.cloned.1.call-done = bf16[128,6144]{1,0:T(8,128)(2,1)} async-done(((bf16[512,6144]{1,0:T(8,128)(2,1)}), bf16[128,6144]{1,0:T(8,128)(2,1)}) %reduce-scatter.2.cloned.1.call-update) | async-done | bytes 1572880 | tf_op jit(solution)/shard_map/reduce_scatter | solution.py:128
  (269 shorter events, 94.7 us)
Async XLA Ops:
  6.5 51.5 %copy-start = (bf16[6144,128]{1,0:T(8,128)(2,1)S(1)}, bf16[6144,128]{1,0:T(8,128)(2,1)}, u32[]{:S(2)}) copy-start(bf16[6144,128]{1,0:T(8,128)(2,1)} %param.14) | copy-start | bytes 4718596
  6.5 0.8 copy-start.3
  6.5 51.5 %all-gather.5.cloned.1.call-start = ((), (), s32[]{:S(2)}) async-start(), calls=%async_computation.1 | async-start | bytes 7864320 | tf_op jit(solution)/shard_map/all_gather | solution.py:30
  7.3 96.7 %all-gather.9.cloned.1.call-start = ((), (), s32[]{:S(2)}) async-start(), calls=%async_computation.4 | async-start | bytes 1179648 | tf_op jit(solution)/shard_map/all_gather | solution.py:90
  7.6 56.9 %copy-start.1 = (f32[2,256]{1,0:T(2,128)}, f32[2,256]{1,0:T(2,128)S(1)}, u32[]{:S(2)}) copy-start(f32[2,256]{1,0:T(2,128)S(1)} %get-tuple-element.626) | copy-start | bytes 6148
  64.3 80.9 %all-gather.7.cloned.1.call-start = ((), (), s32[]{:S(2)}) async-start(), calls=%async_computation.2 | async-start | bytes 1179648 | tf_op jit(solution)/shard_map/all_gather | solution.py:91
  72.1 275.5 %reduce-scatter.2.cloned.1.call-start = ((), (), s32[]{:S(2)}) async-start(), calls=%async_computation.3 | async-start | bytes 7864320 | tf_op jit(solution)/shard_map/reduce_scatter | solution.py:128
  83.4 62.0 %copy-start.2 = (f32[2,256]{1,0:T(2,128)S(1)}, f32[2,256]{1,0:T(2,128)}, u32[]{:S(2)}) copy-start(f32[2,256]{1,0:T(2,128)} %copy-done.1) | copy-start | bytes 6148
Sparse Core Ops, SparseCore 0:
  8.9 49.0 all-gather.4
  64.4 39.5 all-gather.8
  106.1 39.0 all-gather.6
  290.4 57.1 reduce-scatter.1
where the time goes:
time: 357 us; the launch traced here: 354 us
  waiting for transfers between devices  168 us (47%)
  matrix products  68.1 us (19%)
  loops' own time  38.8 us (11%)
  other arithmetic  32.9 us (9%)
  local copies, waits for them, and re-layouts  32.2 us (9%)
  between operations  13.3 us (4%)
    reduce_scatter x1, waiting for transfers between devices, body(): lax.psum_scatter(jnp.dot(heads_out, w_out, preferred_element_type=jnp.flo...  57.3 us
    all_gather x1, waiting for transfers between devices, body(): piece = lax.all_gather(tokens, 'tp', axis=0, tiled=True)  50.4 us
    all_gather x1, waiting for transfers between devices, body(): value_piece = lax.all_gather(value_rows, 'ctx', axis=0, tiled=True)  41.2 us
    another operation x1, loops' own time, body(): folded = lax.fori_loop(0, count // tile, one_tile, initial)  37.6 us
    dot_general x17, matrix products, update(): lax.dot_general(query_c, key_tile, (((1,), (1,)), ((), ())), preferred_el...  23.4 us
    reduce_min x16, other arithmetic, one_tile(): needed = jnp.min(pos_tile) <= jnp.max(pos_c)  21.5 us
    all_gather x1, waiting for transfers between devices, body(): key_piece = lax.all_gather(key, 'ctx', axis=0, tiled=True)  18.8 us
    dynamic_slice x32, local copies, waits for them, and re-layouts, one_tile(): key_tile = lax.dynamic_slice_in_dim(key_piece, step * tile, tile, 0)  15.3 us
  transfers between devices with their start and end apart: 4, of which 4 were waited for; matrix products, arithmetic and copies ran while one was open for 6% of the time, Pallas kernels for 0%

commit v1 on v0

v1 whole, which is shorter than its diff:
```python
import functools
import math

import jax
import jax.numpy as jnp
from jax import lax
from jax.experimental import pallas as pl
from jax.experimental.pallas import tpu as pltpu
from jax.sharding import PartitionSpec as P

ROPE_BASE = 1000000.0


def rotary_embed(values, token_positions):
    half = values.shape[-1] // 2
    freq = ROPE_BASE ** (-(jnp.arange(half, dtype=jnp.float32) * 2.0) / values.shape[-1])
    angle = token_positions[:, None] * freq[None, :]
    cosine = jnp.cos(angle)[:, None, :]
    sine = jnp.sin(angle)[:, None, :]
    first = values[..., :half]
    second = values[..., half:]
    return jnp.concatenate(
        [first * cosine - second * sine, second * cosine + first * sine], axis=-1
    )


LOG2_E = 1.4426950408889634


def attend_kernel(mine_ref, slots_ref, q_ref, kv_ref, o_ref, top_ref, total_ref, accum_ref):
    dim = kv_ref.shape[1] // 2
    span = q_ref.shape[0] // 2
    group = q_ref.shape[1] // dim
    parts = span // dim
    factor = LOG2_E / math.sqrt(dim)

    def tile(slot, half, first):
        start = pl.multiple_of(slot * span, span)
        key = kv_ref[pl.ds(start, span), :dim]
        value = kv_ref[pl.ds(start, span), dim:]
        if first:
            keep = lax.broadcasted_iota(jnp.int32, (span, span), 1) <= lax.broadcasted_iota(
                jnp.int32, (span, span), 0
            )
        for head in range(group):
            query = q_ref[half * span : (half + 1) * span, head * dim : (head + 1) * dim]
            score = lax.dot_general(
                query, key, (((1,), (1,)), ((), ())), preferred_element_type=jnp.float32
            )
            if first:
                score = jnp.where(keep, score, -1e30)
            top = jnp.broadcast_to(jnp.max(score, axis=1, keepdims=True), (span, dim))
            if not first:
                old = top_ref[head]
                top = jnp.maximum(old, top)
            weights = [
                jnp.exp2((score[:, part * dim : (part + 1) * dim] - top) * factor)
                for part in range(parts)
            ]
            total = functools.reduce(jnp.add, weights)
            weight = jnp.concatenate(weights, axis=1).astype(jnp.bfloat16)
            mixed = jnp.dot(weight, value, preferred_element_type=jnp.float32)
            if not first:
                scale = jnp.exp2((old - top) * factor)
                total = total_ref[head] * scale + total
                mixed = accum_ref[head] * scale + mixed
            top_ref[head] = top
            total_ref[head] = total
            accum_ref[head] = mixed

    for half in range(2):
        tile(2 * mine_ref[2] + half, half, True)

        def step(index, carry):
            tile(slots_ref[index], half, False)
            return carry

        lax.fori_loop(0, mine_ref[half], step, 0)
        for head in range(group):
            total = jnp.sum(total_ref[head], axis=1, keepdims=True)
            o_ref[half * span : (half + 1) * span, head * dim : (head + 1) * dim] = (
                accum_ref[head] / total
            ).astype(o_ref.dtype)


def attend(span_order, rank, query, kv):
    rows, columns = query.shape
    dim = kv.shape[1] // 2
    span = rows // 2
    group = columns // dim
    flat = span_order.reshape(-1)
    index = jnp.arange(flat.shape[0], dtype=jnp.int32)
    slots = jnp.sum(jnp.where(flat[None, :] == index[:, None], index[None, :], 0), axis=1)
    mine = lax.dynamic_slice(span_order, (rank, jnp.int32(0)), (1, 2)).reshape(2)
    mine = jnp.concatenate([mine, rank.astype(jnp.int32)[None]])
    return pl.pallas_call(
        attend_kernel,
        out_shape=jax.ShapeDtypeStruct((rows, columns), jnp.bfloat16),
        in_specs=[pl.BlockSpec(memory_space=pltpu.SMEM)] * 2
        + [pl.BlockSpec(memory_space=pltpu.VMEM)] * 2,
        out_specs=pl.BlockSpec(memory_space=pltpu.VMEM),
        scratch_shapes=[pltpu.VMEM((group, span, dim), jnp.float32)] * 3,
        compiler_params=pltpu.CompilerParams(vmem_limit_bytes=40 * 2**20),
        name="attend",
    )(mine, slots, query, kv)


def body(tokens, w_query, key_matrix, value_matrix, w_out, span_order):
    rank = lax.axis_index("ctx")
    head_dim = key_matrix.shape[1]
    qcols = w_query.shape[1]
    group = qcols // head_dim
    piece = lax.all_gather(tokens, "tp", axis=0, tiled=True)
    block_rows = piece.shape[0]
    span = block_rows // 2
    mine = lax.dynamic_slice(span_order, (rank, jnp.int32(0)), (1, 2)).reshape(2)
    own_pos = (
        (mine[:, None] * span + jnp.arange(span, dtype=jnp.int32)[None, :])
        .reshape(-1)
        .astype(jnp.float32)
    )
    key = jnp.dot(piece, key_matrix, preferred_element_type=jnp.float32)
    value = jnp.dot(piece, value_matrix, preferred_element_type=jnp.float32).astype(jnp.bfloat16)
    key = (
        rotary_embed(key.reshape(block_rows, 1, head_dim), own_pos)
        .reshape(block_rows, head_dim)
        .astype(jnp.bfloat16)
    )
    kv = lax.all_gather(jnp.concatenate([key, value], axis=1), "ctx", axis=0, tiled=True)
    query = jnp.dot(piece, w_query, preferred_element_type=jnp.float32)
    query = (
        rotary_embed(query.reshape(block_rows, group, head_dim), own_pos)
        .astype(jnp.bfloat16)
        .reshape(block_rows, qcols)
    )
    heads_out = attend(span_order, rank, query, kv)
    return lax.psum_scatter(
        jnp.dot(heads_out, w_out, preferred_element_type=jnp.float32).astype(jnp.bfloat16),
        "tp",
        scatter_dimension=0,
        tiled=True,
    )


def solution(mesh):
    return jax.shard_map(
        body,
        mesh=mesh,
        in_specs=(
            P(("ctx", "tp"), None),
            P(None, "tp"),
            P(None, "tp"),
            P(None, "tp"),
            P("tp", None),
            P(),
        ),
        out_specs=P(("ctx", "tp"), None),
        check_vma=False,
    )
```

time: 357 us -> 210 us (0.59)
  matrix products: 68.1 us -> 26.7 us
  loops' own time: 38.8 us -> 0 us
  other arithmetic: 32.9 us -> 3.2 us
  local copies, waits for them, and re-layouts: 32.2 us -> 3.08 us
  waiting for transfers between devices: 168 us -> 146 us
  Pallas kernels: 0 us -> 18 us
    another operation x33 -> x0, loops' own time: 38.8 us -> none  [the longest x1 37.6 us: body(): folded = lax.fori_loop(0, count // tile, one_tile, initial)]
    dot_general x36 -> x2, matrix products: 51.7 us -> 14.3 us  [the longest x1 9.56 us: body(): query = jnp.dot(piece, w_query, preferred_element_type=jnp.float32)]
    dynamic_slice x48 -> x1, local copies, waits for them, and re-layouts: 28.9 us -> 1.03 us  [attend(): lax.dynamic_slice(span_order, (rank, jnp.int32(0)), (1, 2)).reshape(2)]
    all_gather x2 -> x1, waiting for transfers between devices: 60 us -> 38.3 us  [body(): lax.all_gather(jnp.concatenate([key, value], axis=1), 'ctx', axis=0, tile...]
    reduce_min x16 -> x0, other arithmetic: 21.5 us -> none  [one_tile(): needed = jnp.min(pos_tile) <= jnp.max(pos_c)]
    pallas_call x0 -> x1, Pallas kernels: none -> 18 us  [attend(): pl.pallas_call(attend_kernel, out_shape=jax.ShapeDtypeStruct((rows, colum...]
    reduce_sum x18 -> x1, other arithmetic: 5.98 us -> 0.11 us  [attend(): jnp.sum(jnp.where(flat[None, :] == index[:, None], index[None, :], 0), ax...]
    dot_general x1, matrix products: 5.65 us -> 1.81 us  [body(): jnp.dot(piece, value_matrix, preferred_element_type=jnp.float32)]
  transfers between devices with their start and end apart: 4 -> 3, of which waited for: 4 -> 3; matrix products, arithmetic and copies ran while one was open for 6% -> 6% of each run, Pallas kernels for 0% -> 0%
where the time goes in v1:
time: 210 us
  waiting for transfers between devices  146 us (70%)
  matrix products  26.7 us (13%)
  Pallas kernels  18 us (9%)
  between operations  13.2 us (6%)
  other arithmetic  3.2 us (2%)
  local copies, waits for them, and re-layouts  3.08 us (1%)
    reduce_scatter x1, waiting for transfers between devices, body(): lax.psum_scatter(jnp.dot(heads_out, w_out, preferred_element_type=jnp.flo...  57 us
    all_gather x1, waiting for transfers between devices, body(): piece = lax.all_gather(tokens, 'tp', axis=0, tiled=True)  49.6 us
    all_gather x1, waiting for transfers between devices, body(): lax.all_gather(jnp.concatenate([key, value], axis=1), 'ctx', axis=0, tile...  38.3 us
    pallas_call x1, Pallas kernels, attend(): pl.pallas_call(attend_kernel, out_shape=jax.ShapeDtypeStruct((rows, colum...  18 us
    dot_general x1, matrix products, body(): jnp.dot(heads_out, w_out, preferred_element_type=jnp.float32)  10.6 us
    dot_general x1, matrix products, body(): query = jnp.dot(piece, w_query, preferred_element_type=jnp.float32)  9.56 us
    dot_general x1, matrix products, body(): key = jnp.dot(piece, key_matrix, preferred_element_type=jnp.float32)  4.72 us
  transfers between devices with their start and end apart: 3, of which 3 were waited for; matrix products, arithmetic and copies ran while one was open for 6% of the time, Pallas kernels for 0%

profile of v1, /device:TPU:0, one launch (start us, length us, event | category | flops | bytes accessed | tf_op | source)
XLA Modules:
  0.0 210.0 jit_solution(10577566463977650642)
XLA Ops:
  6.5 0.0 copy-start
  6.5 0.0 all-gather.3.cloned.1.call-start
  6.5 0.7 all-gather.3.cloned.1.call-update
  7.3 0.0 all-gather.5.cloned.1.call-start
  7.3 1.0 dynamic-slice_reduce_fusion
  8.3 0.1 convert_bitcast_fusion
  8.4 49.6 %all-gather.3.cloned.1.call-done = bf16[512,6144]{1,0:T(8,128)(2,1)} async-done(((bf16[128,6144]{1,0:T(8,128)(2,1)}), bf16[512,6144]{1,0:T(8,128)(2,1)}) %all-gather.3.cloned.1.call-update) | async-done | bytes 6291472 | tf_op jit(solution)/shard_map/all_gather | solution.py:113
  58.0 0.0 copy-done
  58.0 4.7 %convolution_bitcast_fusion = f32[512,1,128]{2,0,1:T(8,128)S(1)} fusion(bf16[512,6144]{1,0:T(8,128)(2,1)} %all-gather.3.cloned.1.call-done, bf16[6144,128]{1,0:T(8,128)(2,1)S(1)} %copy-done), kind=kOutput, calls=%fused_computation.1 | convolution fusion | flops 805306368 | bytes 8126464 | tf_op jit(solution)/shard_map/dot_general | solution.py:122
  62.8 0.0 copy-start.2
  62.8 1.2 fusion.5
  64.0 0.1 maximum_bitcast_fusion
  64.1 1.8 convolution_convert_fusion.1
  66.0 0.7 pad_maximum_fusion.1
  66.7 0.0 all-gather.5.cloned.1.call-update
  66.7 0.0 reduce-scatter.2.cloned.1.call-start
  66.8 0.0 copy-done.2
  66.8 0.1 copy.18
  66.9 0.1 eq.15
  66.9 0.1 pad_add_fusion.mine_ref
  67.0 0.1 select_reduce_fusion.slots_ref
  67.1 0.5 multiply_cosine_fusion.1
  67.7 9.6 %fusion.8 = f32[512,768]{0,1:T(8,128)S(1)} fusion(bf16[512,6144]{1,0:T(8,128)(2,1)} %all-gather.3.cloned.1.call-done, bf16[6144,768]{1,0:T(8,128)(2,1)} %param.7), kind=kOutput, calls=%fused_computation.27 | convolution fusion | flops 4831838208 | bytes 17301504 | tf_op jit(solution)/shard_map/dot_general | solution.py:130
  77.2 0.3 subtract_convert_fusion
  77.5 0.1 pad_maximum_fusion
  77.6 0.3 copy.23.q_ref
  77.8 38.3 %all-gather.5.cloned.1.call-done.kv_ref = bf16[4096,256]{1,0:T(8,128)(2,1)} async-done(((bf16[512,256]{1,0:T(8,128)(2,1)}), bf16[4096,256]{1,0:T(8,128)(2,1)}) %all-gather.5.cloned.1.call-update) | async-done | bytes 2097168 | tf_op jit(solution)/shard_map/all_gather | solution.py:129
  116.2 1.6 copy-done.1
  117.8 18.0 %attend.1 = bf16[512,768]{1,0:T(8,128)(2,1)S(1)} custom-call(s32[3]{0:T(128)S(1)} %pad_add_fusion.mine_ref, s32[16]{0:T(128)S(1)} %select_reduce_fusion.slots_ref, bf16[512,768]{1,0:T(8,128)(2,1)S(1)} %copy.23.q_ref, bf16[4096,256]{1,0:T(8,128)(2,1)S(1)} %copy-done.1), custom_call_target="tpu_custom_call" | custom-call | tf_op jit(solution)/shard_map/attend/pallas_call | solution.py:96
  135.8 10.6 %convolution_convert_fusion = bf16[512,6144]{1,0:T(8,128)(2,1)} fusion(bf16[512,768]{1,0:T(8,128)(2,1)S(1)} %attend.1, bf16[768,6144]{1,0:T(8,128)(2,1)} %param.10), kind=kOutput, calls=%fused_computation | convolution fusion | flops 4834983936 | bytes 16515072 | tf_op jit(solution)/shard_map/dot_general | solution.py:138
  146.4 0.0 reduce-scatter.2.cloned.1.call-update
  146.4 57.0 %reduce-scatter.2.cloned.1.call-done = bf16[128,6144]{1,0:T(8,128)(2,1)} async-done(((bf16[512,6144]{1,0:T(8,128)(2,1)}), bf16[128,6144]{1,0:T(8,128)(2,1)}) %reduce-scatter.2.cloned.1.call-update) | async-done | bytes 1572880 | tf_op jit(solution)/shard_map/reduce_scatter | solution.py:137
  (8 shorter events, 0.0 us)
Async XLA Ops:
  6.5 51.5 %copy-start = (bf16[6144,128]{1,0:T(8,128)(2,1)S(1)}, bf16[6144,128]{1,0:T(8,128)(2,1)}, u32[]{:S(2)}) copy-start(bf16[6144,128]{1,0:T(8,128)(2,1)} %param.8) | copy-start | bytes 4718596
  6.5 57.6 %copy-start.4 = (bf16[6144,128]{1,0:T(8,128)(2,1)S(1)}, bf16[6144,128]{1,0:T(8,128)(2,1)}, u32[]{:S(2)}) copy-start(bf16[6144,128]{1,0:T(8,128)(2,1)} %param.9) | copy-start | bytes 4718596
  6.5 51.5 %all-gather.3.cloned.1.call-start = ((), (), s32[]{:S(2)}) async-start(), calls=%async_computation.1 | async-start | bytes 7864320 | tf_op jit(solution)/shard_map/all_gather | solution.py:113
  7.3 108.9 %all-gather.5.cloned.1.call-start = ((), (), s32[]{:S(2)}) async-start(), calls=%async_computation.2 | async-start | bytes 2359296 | tf_op jit(solution)/shard_map/all_gather | solution.py:129
  58.0 6.1 %copy-start.3 = (bf16[512,6144]{1,0:T(8,128)(2,1)S(1)}, bf16[512,6144]{1,0:T(8,128)(2,1)}, u32[]{:S(2)}) copy-start(bf16[512,6144]{1,0:T(8,128)(2,1)} %all-gather.3.cloned.1.call-done) | copy-start | bytes 18874372
  62.8 4.0 %copy-start.2 = (s32[8,2]{0,1:T(2,128)S(1)}, s32[8,2]{0,1:T(2,128)}, u32[]{:S(2)}) copy-start(s32[8,2]{0,1:T(2,128)} %param.11) | copy-start | bytes 196
  66.7 136.7 %reduce-scatter.2.cloned.1.call-start = ((), (), s32[]{:S(2)}) async-start(), calls=%async_computation.3 | async-start | bytes 7864320 | tf_op jit(solution)/shard_map/reduce_scatter | solution.py:137
  116.2 1.6 copy-start.1
Sparse Core Ops, SparseCore 0:
  8.9 49.0 all-gather.2
  66.8 49.2 all-gather.4
  146.6 56.8 reduce-scatter.1

commit v2 on v1

--- a/solution.py
+++ b/solution.py
@@ -9,19 +9,6 @@
 from jax.sharding import PartitionSpec as P
 
 ROPE_BASE = 1000000.0
-
-
-def rotary_embed(values, token_positions):
-    half = values.shape[-1] // 2
-    freq = ROPE_BASE ** (-(jnp.arange(half, dtype=jnp.float32) * 2.0) / values.shape[-1])
-    angle = token_positions[:, None] * freq[None, :]
-    cosine = jnp.cos(angle)[:, None, :]
-    sine = jnp.sin(angle)[:, None, :]
-    first = values[..., :half]
-    second = values[..., half:]
-    return jnp.concatenate(
-        [first * cosine - second * sine, second * cosine + first * sine], axis=-1
-    )
 
 
 LOG2_E = 1.4426950408889634
@@ -105,41 +92,425 @@
     )(mine, slots, query, kv)
 
 
+MESH = pl.DeviceIdType.MESH
+PIECES = 4
+CHUNKS = 8
+
+
+def greet(devices):
+    barrier = pltpu.get_barrier_semaphore()
+    for device in devices:
+        pl.semaphore_signal(barrier, inc=1, device_id=device, device_id_type=MESH)
+    pl.semaphore_wait(barrier, len(devices))
+
+
+def pair_places():
+    place = lax.axis_index("tp")
+    chip = place // 2
+    core = place % 2
+    return chip, core, {"tp": chip * 2 + 1 - core}, {"tp": (1 - chip) * 2 + core}
+
+
+def project_kernel(
+    columns_apart,
+    ranks,
+    tokens_ref,
+    w_query_ref,
+    key_matrix_ref,
+    value_matrix_ref,
+    cosine_ref,
+    sine_ref,
+    query_ref,
+    kv_ref,
+    weights,
+    near,
+    far,
+    kv_near,
+    kv_far,
+    weight_sems,
+    local_sems,
+    near_sems,
+    far_sems,
+    swap_sems,
+    column_sems,
+    row_sems,
+):
+    chip, core, partner, across = pair_places()
+    rank = lax.axis_index("ctx")
+    tall = ranks // columns_apart
+    wide = columns_apart
+    row = rank // wide
+    column = rank % wide
+    count, piece = far.shape[0], far.shape[2]
+    rows, width = tokens_ref.shape
+    dim = key_matrix_ref.shape[1]
+    blocks = weights.shape[0] - 1
+    block = weights.shape[2]
+
+    def along_rows(step):
+        return {"ctx": lax.rem(row + step, tall) * wide + column}
+
+    def along_columns(step):
+        return {"ctx": row * wide + lax.rem(column + step, wide)}
+
+    greet(
+        [partner, across]
+        + [along_rows(step) for step in range(1, tall)]
+        + [along_columns(step) for step in range(1, wide)]
+    )
+
+    def remote(source, target, sems, index, device):
+        return pltpu.make_async_remote_copy(
+            src_ref=source,
+            dst_ref=target,
+            send_sem=sems.at[(0,) + index],
+            recv_sem=sems.at[(1,) + index],
+            device_id=device,
+            device_id_type=MESH,
+        )
+
+    far_copies = []
+    for part in range(count):
+        copy = remote(
+            tokens_ref.at[pl.ds(part * piece, piece)],
+            far.at[part, core],
+            far_sems,
+            (part,),
+            across,
+        )
+        copy.start()
+        far_copies.append(copy)
+    near_copy = remote(tokens_ref, near.at[core], near_sems, (), partner)
+    near_copy.start()
+    own_copy = pltpu.make_async_copy(tokens_ref, near.at[core], local_sems.at[0])
+    own_copy.start()
+    loads = [
+        pltpu.make_async_copy(
+            key_matrix_ref, weights.at[blocks, :, pl.ds(0, dim)], weight_sems.at[blocks]
+        ),
+        pltpu.make_async_copy(
+            value_matrix_ref, weights.at[blocks, :, pl.ds(dim, dim)], weight_sems.at[blocks + 1]
+        ),
+    ]
+    for index in range(blocks):
+        loads.append(
+            pltpu.make_async_copy(
+                w_query_ref.at[:, pl.ds(index * block, block)],
+                weights.at[index],
+                weight_sems.at[index],
+            )
+        )
+    for load in loads:
+        load.start()
+
+    def place(part, source):
+        if part == 0:
+            return kv_ref.at[source, chip]
+        return kv_ref.at[source, 1 - chip, :, pl.ds((part - 1) * piece, piece)]
+
+    def tables(part):
+        if part == 0:
+            return cosine_ref[chip], sine_ref[chip]
+        span = slice((part - 1) * piece, part * piece)
+        return cosine_ref[1 - chip, :, span], sine_ref[1 - chip, :, span]
+
+    def flat(values):
+        return values.reshape(values.shape[0] * values.shape[1], values.shape[2])
+
+    def rotate(values, cosine, sine):
+        return values * cosine + pltpu.roll(values, dim // 2, 1) * sine
+
+    waits = []
+
+    def share(part, staged):
+        local = pltpu.make_async_copy(staged, place(part, rank), local_sems.at[1 + part])
+        local.start()
+        waits.append(local.wait)
+        row_copies = []
+        for step in range(1, tall):
+            copy = remote(
+                staged, place(part, rank), row_sems, (part, step - 1), along_rows(step)
+            )
+            copy.start()
+            row_copies.append(copy)
+            waits.append(copy.wait_send)
+        for step in range(1, wide):
+            copy = remote(
+                staged, place(part, rank), column_sems, (part, 0, step - 1), along_columns(step)
+            )
+            copy.start()
+            waits.append(copy.wait_send)
+
+    def pass_on(part):
+        for step in range(1, tall):
+            source = lax.rem(row + tall - step, tall) * wide + column
+            remote(
+                place(part, source),
+                place(part, source),
+                row_sems,
+                (part, step - 1),
+                along_rows(step),
+            ).wait_recv()
+            for side in range(1, wide):
+                copy = remote(
+                    place(part, source),
+                    place(part, source),
+                    column_sems,
+                    (part, step, side - 1),
+                    along_columns(side),
+                )
+                copy.start()
+                waits.append(copy.wait_send)
+
+    def work(part, held, staged):
+        cosine, sine = tables(part)
+        cosine, sine = flat(cosine), flat(sine)
+        both = jnp.dot(flat(held[...]), weights[blocks], preferred_element_type=jnp.float32)
+        key = rotate(both[:, :dim], cosine, sine)
+        kept = jnp.concatenate([key, both[:, dim:]], axis=1).astype(jnp.bfloat16)
+        staged[...] = kept.reshape(staged.shape)
+        share(part, staged)
+        if part == 0:
+            for load in loads[2:]:
+                load.wait()
+
+        def one_block(index, carry):
+            found = jnp.dot(flat(held[...]), weights[index], preferred_element_type=jnp.float32)
+            for head in range(block // dim):
+                turned = rotate(found[:, head * dim : (head + 1) * dim], cosine, sine)
+                turned = turned.astype(jnp.bfloat16).reshape(2, -1, dim)
+                lanes = pl.ds(pl.multiple_of(index * block + head * dim, dim), dim)
+                if part == 0:
+                    query_ref[chip, :, :, lanes] = turned
+                else:
+                    query_ref[1 - chip, :, (part - 1) * piece : part * piece, lanes] = turned
+            return carry
+
+        lax.fori_loop(0, blocks, one_block, 0)
+
+    own_copy.wait()
+    near_copy.wait()
+    for load in loads[:2]:
+        load.wait()
+    work(0, near, kv_near)
+    for part in range(count):
+        far_copies[part].wait_recv()
+        swap = remote(far.at[part, core], far.at[part, core], swap_sems, (part,), partner)
+        swap.start()
+        pass_on(part)
+        swap.wait()
+        work(part + 1, far.at[part], kv_far.at[part])
+    pass_on(count)
+    for copy in far_copies:
+        copy.wait_send()
+    for part in range(count + 1):
+        for step in range(tall):
+            for side in range(1, wide):
+                source = lax.rem(row + tall - step, tall) * wide + lax.rem(
+                    column + wide - side, wide
+                )
+                remote(
+                    place(part, source),
+                    place(part, source),
+                    column_sems,
+                    (part, step, side - 1),
+                    along_columns(side),
+                ).wait_recv()
+    for wait in waits:
+        wait()
+
+
+def project(tokens, w_query, key_matrix, value_matrix, cosine, sine):
+    ranks = lax.axis_size("ctx")
+    wide = 4 if ranks % 16 == 0 else 2
+    rows, width = tokens.shape
+    dim = key_matrix.shape[1]
+    columns = w_query.shape[1]
+    block = 2 * dim
+    blocks = columns // block
+    piece = rows // PIECES
+    dma = pltpu.SemaphoreType.DMA
+    bf16 = jnp.bfloat16
+    return pl.pallas_call(
+        functools.partial(project_kernel, wide, ranks),
+        out_shape=(
+            jax.ShapeDtypeStruct((2, 2, rows, columns), bf16),
+            jax.ShapeDtypeStruct((ranks, 2, 2, rows, 2 * dim), bf16),
+        ),
+        in_specs=[pl.BlockSpec(memory_space=pl.ANY)] * 4
+        + [pl.BlockSpec(memory_space=pltpu.VMEM)] * 2,
+        out_specs=(pl.BlockSpec(memory_space=pltpu.VMEM), pl.BlockSpec(memory_space=pl.ANY)),
+        scratch_shapes=[
+            pltpu.VMEM((blocks + 1, width, block), bf16),
+            pltpu.VMEM((2, rows, width), bf16),
+            pltpu.VMEM((PIECES, 2, piece, width), bf16),
+            pltpu.VMEM((2, rows, block), bf16),
+            pltpu.VMEM((PIECES, 2, piece, block), bf16),
+            dma((blocks + 2,)),
+            dma((PIECES + 2,)),
+            dma((2,)),
+            dma((2, PIECES)),
+            dma((2, PIECES)),
+            dma((2, PIECES + 1, ranks // wide, wide - 1)),
+            dma((2, PIECES + 1, ranks // wide - 1)),
+        ],
+        compiler_params=pltpu.CompilerParams(
+            collective_id=0, has_side_effects=True, vmem_limit_bytes=48 * 2**20
+        ),
+        name="project",
+    )(tokens, w_query, key_matrix, value_matrix, cosine, sine)
+
+
+def combine_kernel(
+    heads_ref,
+    w_ref,
+    out_ref,
+    weights,
+    cross_part,
+    pair_in,
+    cross_out,
+    cross_in,
+    own_part,
+    own_in,
+    weight_sems,
+    pair_sems,
+    cross_sems,
+    own_sems,
+):
+    chip, core, partner, across = pair_places()
+    chunks, _, width = weights.shape
+    rows = out_ref.shape[0]
+    loads = [
+        pltpu.make_async_copy(
+            w_ref.at[:, pl.ds(index * width, width)], weights.at[index], weight_sems.at[index]
+        )
+        for index in range(chunks)
+    ]
+    for load in loads:
+        load.start()
+    greet([partner, across])
+
+    def remote(source, target, sems, index, device):
+        return pltpu.make_async_remote_copy(
+            src_ref=source,
+            dst_ref=target,
+            send_sem=sems.at[0, index],
+            recv_sem=sems.at[1, index],
+            device_id=device,
+            device_id_type=MESH,
+        )
+
+    def pair_copy(index):
+        return remote(
+            cross_part.at[index, 1 - core], pair_in.at[index], pair_sems, index, partner
+        )
+
+    def cross_copy(index):
+        return remote(cross_out.at[index], cross_in.at[index], cross_sems, index, across)
+
+    def own_copy(index):
+        return remote(own_part.at[index, 1 - core], own_in.at[index], own_sems, index, partner)
+
+    def partial(side, index):
+        heads = heads_ref[side].reshape(2 * rows, heads_ref.shape[3])
+        found = jnp.dot(heads, weights[index], preferred_element_type=jnp.float32)
+        return found.astype(jnp.bfloat16).reshape(2, rows, width)
+
+    def add_pair(index):
+        pair_copy(index).wait_recv()
+        cross_out[index] = (
+            cross_part[index, core].astype(jnp.float32) + pair_in[index].astype(jnp.float32)
+        ).astype(jnp.bfloat16)
+        cross_copy(index).start()
+
+    def first(index, carry):
+        pltpu.make_async_copy(weights.at[index], weights.at[index], weight_sems.at[index]).wait()
+        cross_part[index] = partial(1 - chip, index)
+        pair_copy(index).start()
+
+        @pl.when(index > 0)
+        def _():
+            add_pair(index - 1)
+
+        return carry
+
+    lax.fori_loop(0, chunks, first, 0)
+    add_pair(chunks - 1)
+
+    def second(index, carry):
+        own_part[index] = partial(chip, index)
+        own_copy(index).start()
+        return carry
+
+    lax.fori_loop(0, chunks, second, 0)
+
+    def last(index, carry):
+        own_copy(index).wait()
+        pair_copy(index).wait_send()
+        cross_copy(index).wait()
+        total = own_part[index, core].astype(jnp.float32) + own_in[index].astype(jnp.float32)
+        total = total + cross_in[index].astype(jnp.float32)
+        out_ref[:, pl.ds(pl.multiple_of(index * width, width), width)] = total.astype(jnp.bfloat16)
+        return carry
+
+    lax.fori_loop(0, chunks, last, 0)
+
+
+def combine(heads_out, w_out):
+    depth, columns = w_out.shape
+    rows = heads_out.shape[0] // 4
+    width = columns // CHUNKS
+    dma = pltpu.SemaphoreType.DMA
+    bf16 = jnp.bfloat16
+    single = pltpu.VMEM((CHUNKS, rows, width), bf16)
+    double = pltpu.VMEM((CHUNKS, 2, rows, width), bf16)
+    return pl.pallas_call(
+        combine_kernel,
+        out_shape=jax.ShapeDtypeStruct((rows, columns), bf16),
+        in_specs=[pl.BlockSpec(memory_space=pltpu.VMEM), pl.BlockSpec(memory_space=pl.ANY)],
+        out_specs=pl.BlockSpec(memory_space=pltpu.VMEM),
+        scratch_shapes=[
+            pltpu.VMEM((CHUNKS, depth, width), bf16),
+            double,
+            single,
+            single,
+            single,
+            double,
+            single,
+            dma((CHUNKS,)),
+            dma((2, CHUNKS)),
+            dma((2, CHUNKS)),
+            dma((2, CHUNKS)),
+        ],
+        compiler_params=pltpu.CompilerParams(
+            collective_id=1, has_side_effects=True, vmem_limit_bytes=48 * 2**20
+        ),
+        name="combine",
+    )(heads_out.reshape(2, 2, rows, depth), w_out)
+
+
 def body(tokens, w_query, key_matrix, value_matrix, w_out, span_order):
     rank = lax.axis_index("ctx")
-    head_dim = key_matrix.shape[1]
-    qcols = w_query.shape[1]
-    group = qcols // head_dim
-    piece = lax.all_gather(tokens, "tp", axis=0, tiled=True)
-    block_rows = piece.shape[0]
-    span = block_rows // 2
+    dim = key_matrix.shape[1]
+    half = dim // 2
+    rows = tokens.shape[0]
+    span = 2 * rows
     mine = lax.dynamic_slice(span_order, (rank, jnp.int32(0)), (1, 2)).reshape(2)
     own_pos = (
         (mine[:, None] * span + jnp.arange(span, dtype=jnp.int32)[None, :])
         .reshape(-1)
         .astype(jnp.float32)
     )
-    key = jnp.dot(piece, key_matrix, preferred_element_type=jnp.float32)
-    value = jnp.dot(piece, value_matrix, preferred_element_type=jnp.float32).astype(jnp.bfloat16)
-    key = (
-        rotary_embed(key.reshape(block_rows, 1, head_dim), own_pos)
-        .reshape(block_rows, head_dim)
-        .astype(jnp.bfloat16)
+    freq = ROPE_BASE ** (-(jnp.arange(half, dtype=jnp.float32) * 2.0) / dim)
+    angle = own_pos[:, None] * freq[None, :]
+    cosine, sine = jnp.cos(angle), jnp.sin(angle)
+    cosine = jnp.concatenate([cosine, cosine], axis=1).reshape(2, 2, rows, dim)
+    sine = jnp.concatenate([-sine, sine], axis=1).reshape(2, 2, rows, dim)
+    query, kv = project(tokens, w_query, key_matrix, value_matrix, cosine, sine)
+    heads_out = attend(
+        span_order, rank, query.reshape(4 * rows, -1), kv.reshape(-1, 2 * dim)
     )
-    kv = lax.all_gather(jnp.concatenate([key, value], axis=1), "ctx", axis=0, tiled=True)
-    query = jnp.dot(piece, w_query, preferred_element_type=jnp.float32)
-    query = (
-        rotary_embed(query.reshape(block_rows, group, head_dim), own_pos)
-        .astype(jnp.bfloat16)
-        .reshape(block_rows, qcols)
-    )
-    heads_out = attend(span_order, rank, query, kv)
-    return lax.psum_scatter(
-        jnp.dot(heads_out, w_out, preferred_element_type=jnp.float32).astype(jnp.bfloat16),
-        "tp",
-        scatter_dimension=0,
-        tiled=True,
-    )
+    return combine(heads_out, w_out)
 
 
 def solution(mesh):

time: 210 us -> 118 us (0.56)
  waiting for transfers between devices: 146 us -> 0 us
  Pallas kernels: 18 us -> 109 us
  matrix products: 26.7 us -> 0 us
  between operations: 13.2 us -> 0.07 us
  local copies, waits for them, and re-layouts: 3.08 us -> 7.36 us
    pallas_call x0 -> x2, Pallas kernels: none -> 90.7 us  [the longest x1 52.1 us: project(): pl.pallas_call(functools.partial(project_kernel, wide, ranks), out_shape=...]
    all_gather x2 -> x0, waiting for transfers between devices: 87.9 us -> none  [the longest x1 49.6 us: body(): piece = lax.all_gather(tokens, 'tp', axis=0, tiled=True)]
    reduce_scatter x1 -> x0, waiting for transfers between devices: 57 us -> none  [body(): lax.psum_scatter(jnp.dot(heads_out, w_out, preferred_element_type=jnp.flo...]
    dot_general x4 -> x0, matrix products: 26.7 us -> none  [the longest x1 10.6 us: body(): jnp.dot(heads_out, w_out, preferred_element_type=jnp.float32)]
    unnamed x12 -> x10, local copies, waits for them, and re-layouts: 1.7 us -> 6.3 us
  transfers between devices with their start and end apart: 3 -> 0, of which waited for: 3 -> 0; matrix products, arithmetic and copies ran while one was open for 6% -> 0% of each run, Pallas kernels for 0% -> 0%
where the time goes in v2:
time: 118 us; the launch traced here: 117 us
  Pallas kernels  109 us (92%)
  local copies, waits for them, and re-layouts  7.36 us (6%)
  other arithmetic  1.48 us (1%)
    pallas_call x1, Pallas kernels, project(): pl.pallas_call(functools.partial(project_kernel, wide, ranks), out_shape=...  52.1 us
    pallas_call x1, Pallas kernels, combine(): pl.pallas_call(combine_kernel, out_shape=jax.ShapeDtypeStruct((rows, colu...  38.6 us
    pallas_call x1, Pallas kernels, attend(): pl.pallas_call(attend_kernel, out_shape=jax.ShapeDtypeStruct((rows, colum...  17.9 us
    unnamed x10, local copies, waits for them, and re-layouts  6.3 us

profile of v2, /device:TPU:0, one launch (start us, length us, event | category | flops | bytes accessed | tf_op | source)
XLA Modules:
  0.0 117.5 jit_solution(4052773230872326845)
XLA Ops:
  0.0 0.0 copy-start.1
  0.0 1.0 dynamic-slice_reduce_fusion
  1.0 0.1 pad_add_fusion.mine_ref
  1.1 0.1 add_convert_fusion
  1.2 0.8 copy.9
  1.9 0.1 eq.15
  2.0 0.1 select_reduce_fusion.slots_ref
  2.1 1.0 fusion
  3.1 0.2 pad_maximum_fusion
  3.3 0.0 copy-done.1
  3.3 0.0 copy-start.2
  3.3 1.4 %copy-done.2 = bf16[6144,128]{1,0:T(8,128)(2,1)S(1)} copy-done((bf16[6144,128]{1,0:T(8,128)(2,1)S(1)}, bf16[6144,128]{1,0:T(8,128)(2,1)}, u32[]{:S(2)}) %copy-start.2) | copy-done | bytes 1572888
  4.7 0.0 copy-start.3
  4.7 1.4 %copy-done.3 = bf16[6144,128]{1,0:T(8,128)(2,1)S(1)} copy-done((bf16[6144,128]{1,0:T(8,128)(2,1)S(1)}, bf16[6144,128]{1,0:T(8,128)(2,1)}, u32[]{:S(2)}) %copy-start.3) | copy-done | bytes 1572888
  6.2 52.1 %project.1 = (bf16[2,2,128,768]{3,2,1,0:T(8,128)(2,1)S(1)}, bf16[8,2,2,128,256]{4,3,2,1,0:T(8,128)(2,1)}) custom-call(bf16[128,6144]{1,0:T(8,128)(2,1)S(1)} %copy-done.1, bf16[6144,768]{1,0:T(8,128)(2,1)} %w_query_ref.1, bf16[6144,128]{1,0:T(8,128)(2,1)S(1)} %copy-done.2, bf16[6144,128]{1,0:T(8,128)(2,1)S(1)} %copy-done.3, ...), custom_call_target="tpu_custom_call" | custom-call | tf_op jit(solution)/shard_map/project/pallas_call | solution.py:334
  58.2 0.0 copy-start
  58.2 1.6 %copy-done = bf16[8,2,2,128,256]{4,3,2,1,0:T(8,128)(2,1)S(1)} copy-done((bf16[8,2,2,128,256]{4,3,2,1,0:T(8,128)(2,1)S(1)}, bf16[8,2,2,128,256]{4,3,2,1,0:T(8,128)(2,1)}, u32[]{:S(2)}) %copy-start) | copy-done | bytes 2097176
  59.8 17.9 %attend.1 = bf16[512,768]{1,0:T(8,128)(2,1)S(1)} custom-call(s32[3]{0:T(128)S(1)} %pad_add_fusion.mine_ref, s32[16]{0:T(128)S(1)} %select_reduce_fusion.slots_ref, bf16[512,768]{1,0:T(8,128)(2,1)S(1)} %bitcast.6, bf16[4096,256]{1,0:T(8,128)(2,1)S(1)} %bitcast.5), custom_call_target="tpu_custom_call" | custom-call | tf_op jit(solution)/shard_map/attend/pallas_call | solution.py:83
  77.7 38.6 %combine.1 = bf16[128,6144]{1,0:T(8,128)(2,1)S(1)} custom-call(bf16[2,2,128,768]{3,2,1,0:T(8,128)(2,1)S(1)} %bitcast.4, bf16[768,6144]{1,0:T(8,128)(2,1)} %w_ref.1), custom_call_target="tpu_custom_call" | custom-call | tf_op jit(solution)/shard_map/combine/pallas_call | solution.py:467
  116.3 1.1 copy.11
  (2 shorter events, 0.0 us)
Async XLA Ops:
  0.0 3.3 %copy-start.1 = (bf16[128,6144]{1,0:T(8,128)(2,1)S(1)}, bf16[128,6144]{1,0:T(8,128)(2,1)}, u32[]{:S(2)}) copy-start(bf16[128,6144]{1,0:T(8,128)(2,1)} %tokens_ref.1) | copy-start | bytes 4718596
  3.3 1.4 %copy-start.2 = (bf16[6144,128]{1,0:T(8,128)(2,1)S(1)}, bf16[6144,128]{1,0:T(8,128)(2,1)}, u32[]{:S(2)}) copy-start(bf16[6144,128]{1,0:T(8,128)(2,1)} %key_matrix_ref.1) | copy-start | bytes 4718596
  4.7 1.4 %copy-start.3 = (bf16[6144,128]{1,0:T(8,128)(2,1)S(1)}, bf16[6144,128]{1,0:T(8,128)(2,1)}, u32[]{:S(2)}) copy-start(bf16[6144,128]{1,0:T(8,128)(2,1)} %value_matrix_ref.1) | copy-start | bytes 4718596
  58.2 1.6 %copy-start = (bf16[8,2,2,128,256]{4,3,2,1,0:T(8,128)(2,1)S(1)}, bf16[8,2,2,128,256]{4,3,2,1,0:T(8,128)(2,1)}, u32[]{:S(2)}) copy-start(bf16[8,2,2,128,256]{4,3,2,1,0:T(8,128)(2,1)} %get-tuple-element.8) | copy-start | bytes 6291460

commit v3 on v2

--- a/solution.py
+++ b/solution.py
@@ -14,87 +14,10 @@
 LOG2_E = 1.4426950408889634
 
 
-def attend_kernel(mine_ref, slots_ref, q_ref, kv_ref, o_ref, top_ref, total_ref, accum_ref):
-    dim = kv_ref.shape[1] // 2
-    span = q_ref.shape[0] // 2
-    group = q_ref.shape[1] // dim
-    parts = span // dim
-    factor = LOG2_E / math.sqrt(dim)
-
-    def tile(slot, half, first):
-        start = pl.multiple_of(slot * span, span)
-        key = kv_ref[pl.ds(start, span), :dim]
-        value = kv_ref[pl.ds(start, span), dim:]
-        if first:
-            keep = lax.broadcasted_iota(jnp.int32, (span, span), 1) <= lax.broadcasted_iota(
-                jnp.int32, (span, span), 0
-            )
-        for head in range(group):
-            query = q_ref[half * span : (half + 1) * span, head * dim : (head + 1) * dim]
-            score = lax.dot_general(
-                query, key, (((1,), (1,)), ((), ())), preferred_element_type=jnp.float32
-            )
-            if first:
-                score = jnp.where(keep, score, -1e30)
-            top = jnp.broadcast_to(jnp.max(score, axis=1, keepdims=True), (span, dim))
-            if not first:
-                old = top_ref[head]
-                top = jnp.maximum(old, top)
-            weights = [
-                jnp.exp2((score[:, part * dim : (part + 1) * dim] - top) * factor)
-                for part in range(parts)
-            ]
-            total = functools.reduce(jnp.add, weights)
-            weight = jnp.concatenate(weights, axis=1).astype(jnp.bfloat16)
-            mixed = jnp.dot(weight, value, preferred_element_type=jnp.float32)
-            if not first:
-                scale = jnp.exp2((old - top) * factor)
-                total = total_ref[head] * scale + total
-                mixed = accum_ref[head] * scale + mixed
-            top_ref[head] = top
-            total_ref[head] = total
-            accum_ref[head] = mixed
-
-    for half in range(2):
-        tile(2 * mine_ref[2] + half, half, True)
-
-        def step(index, carry):
-            tile(slots_ref[index], half, False)
-            return carry
-
-        lax.fori_loop(0, mine_ref[half], step, 0)
-        for head in range(group):
-            total = jnp.sum(total_ref[head], axis=1, keepdims=True)
-            o_ref[half * span : (half + 1) * span, head * dim : (head + 1) * dim] = (
-                accum_ref[head] / total
-            ).astype(o_ref.dtype)
-
-
-def attend(span_order, rank, query, kv):
-    rows, columns = query.shape
-    dim = kv.shape[1] // 2
-    span = rows // 2
-    group = columns // dim
-    flat = span_order.reshape(-1)
-    index = jnp.arange(flat.shape[0], dtype=jnp.int32)
-    slots = jnp.sum(jnp.where(flat[None, :] == index[:, None], index[None, :], 0), axis=1)
-    mine = lax.dynamic_slice(span_order, (rank, jnp.int32(0)), (1, 2)).reshape(2)
-    mine = jnp.concatenate([mine, rank.astype(jnp.int32)[None]])
-    return pl.pallas_call(
-        attend_kernel,
-        out_shape=jax.ShapeDtypeStruct((rows, columns), jnp.bfloat16),
-        in_specs=[pl.BlockSpec(memory_space=pltpu.SMEM)] * 2
-        + [pl.BlockSpec(memory_space=pltpu.VMEM)] * 2,
-        out_specs=pl.BlockSpec(memory_space=pltpu.VMEM),
-        scratch_shapes=[pltpu.VMEM((group, span, dim), jnp.float32)] * 3,
-        compiler_params=pltpu.CompilerParams(vmem_limit_bytes=40 * 2**20),
-        name="attend",
-    )(mine, slots, query, kv)
-
-
 MESH = pl.DeviceIdType.MESH
 PIECES = 4
-CHUNKS = 8
+STRIPS = 4
+CHUNKS = 4
 
 
 def greet(devices):
@@ -355,31 +278,53 @@
             dma((2, PIECES + 1, ranks // wide - 1)),
         ],
         compiler_params=pltpu.CompilerParams(
-            collective_id=0, has_side_effects=True, vmem_limit_bytes=48 * 2**20
+            collective_id=0, has_side_effects=True, vmem_limit_bytes=60 * 2**20
         ),
         name="project",
     )(tokens, w_query, key_matrix, value_matrix, cosine, sine)
 
 
 def combine_kernel(
-    heads_ref,
+    ranks,
+    spans_ref,
+    query_ref,
+    kv_hbm_ref,
     w_ref,
     out_ref,
+    kv_ref,
     weights,
+    queries,
+    tops,
+    totals,
+    accums,
+    heads_out,
     cross_part,
     pair_in,
     cross_out,
     cross_in,
     own_part,
     own_in,
+    kv_sem,
     weight_sems,
     pair_sems,
     cross_sems,
     own_sems,
 ):
     chip, core, partner, across = pair_places()
+    rank = lax.axis_index("ctx")
     chunks, _, width = weights.shape
-    rows = out_ref.shape[0]
+    rows = query_ref.shape[2]
+    span = 2 * rows
+    dim = kv_ref.shape[1] // 2
+    strip = heads_out.shape[0] // 2
+    strips = rows // strip
+    sets, stacked, _ = queries.shape
+    group = stacked // (2 * strip)
+    parts = span // dim
+    factor = LOG2_E / math.sqrt(dim)
+
+    kv_load = pltpu.make_async_copy(kv_hbm_ref, kv_ref, kv_sem)
+    kv_load.start()
     loads = [
         pltpu.make_async_copy(
             w_ref.at[:, pl.ds(index * width, width)], weights.at[index], weight_sems.at[index]
@@ -389,6 +334,7 @@
     for load in loads:
         load.start()
     greet([partner, across])
+    kv_load.wait()
 
     def remote(source, target, sems, index, device):
         return pltpu.make_async_remote_copy(
@@ -411,10 +357,92 @@
     def own_copy(index):
         return remote(own_part.at[index, 1 - core], own_in.at[index], own_sems, index, partner)
 
-    def partial(side, index):
-        heads = heads_ref[side].reshape(2 * rows, heads_ref.shape[3])
-        found = jnp.dot(heads, weights[index], preferred_element_type=jnp.float32)
-        return found.astype(jnp.bfloat16).reshape(2, rows, width)
+    def key_tile(slot):
+        start = pl.multiple_of(slot * span, span)
+        return kv_ref[pl.ds(start, span), :dim], kv_ref[pl.ds(start, span), dim:]
+
+    def attend_strip(half, index):
+        start = pl.multiple_of(index * strip, strip)
+        for one in range(sets):
+            for head in range(group):
+                at = (one * group + head) * dim
+                queries[one, head * 2 * strip : (head + 1) * 2 * strip] = query_ref[
+                    half, :, pl.ds(start, strip), at : at + dim
+                ].reshape(2 * strip, dim)
+        own_id = spans_ref[2 * rank + half]
+
+        def tiles(entries, keep):
+            first = keep is not None
+            held = [key_tile(slot) for slot, _ in entries]
+            for one in range(sets):
+                scores = [
+                    lax.dot_general(
+                        queries[one],
+                        key,
+                        (((1,), (1,)), ((), ())),
+                        preferred_element_type=jnp.float32,
+                    )
+                    for key, _ in held
+                ]
+                if first:
+                    scores[0] = jnp.where(keep, scores[0], -1e30)
+                else:
+                    old = tops[one]
+                top = None if first else old
+                for score, (_, away) in zip(scores, entries):
+                    found = jnp.max(score, axis=1, keepdims=True) - away
+                    found = jnp.broadcast_to(found, (stacked, dim))
+                    top = found if top is None else jnp.maximum(top, found)
+                total, mixed = None, None
+                for score, (_, away), (_, value) in zip(scores, entries, held):
+                    base = top + away
+                    weight = [
+                        jnp.exp2((score[:, part * dim : (part + 1) * dim] - base) * factor)
+                        for part in range(parts)
+                    ]
+                    added = functools.reduce(jnp.add, weight)
+                    weight = jnp.concatenate(weight, axis=1).astype(jnp.bfloat16)
+                    product = jnp.dot(weight, value, preferred_element_type=jnp.float32)
+                    total = added if total is None else total + added
+                    mixed = product if mixed is None else mixed + product
+                if not first:
+                    scale = jnp.exp2((old - top) * factor)
+                    total = totals[one] * scale + total
+                    mixed = accums[one] * scale + mixed
+                tops[one] = top
+                totals[one] = total
+                accums[one] = mixed
+
+        def entry(slot):
+            before = jnp.clip(own_id - spans_ref[slot], 0, 1)
+            return slot, (1 - before).astype(jnp.float32) * 1e30
+
+        shape = (group, 2, strip, span)
+        token = (
+            lax.broadcasted_iota(jnp.int32, shape, 1) * rows
+            + lax.broadcasted_iota(jnp.int32, shape, 2)
+            + start
+        )
+        keep = lax.broadcasted_iota(jnp.int32, shape, 3) <= token
+        tiles([(2 * rank + half, 0.0), entry(2 * lax.rem(rank + 1 - half, ranks))], keep.reshape(stacked, span))
+
+        def step(index, carry):
+            block = lax.rem(rank + half * (1 + index) + (1 - half) * (2 + 2 * index), ranks)
+            later = half + (1 - half) * 2 * lax.rem(rank + 3 + 2 * index, ranks)
+            tiles([entry(2 * block), entry(half * 2 * block + later)], None)
+            return carry
+
+        lax.fori_loop(0, (ranks - 2 + ranks * half) // 2, step, 0)
+        for one in range(sets):
+            total = jnp.sum(totals[one], axis=1, keepdims=True)
+            mixed = (accums[one] / total).astype(jnp.bfloat16)
+            for head in range(group):
+                at = (one * group + head) * dim
+                heads_out[:, at : at + dim] = mixed[head * 2 * strip : (head + 1) * 2 * strip]
+
+    def partial(index):
+        found = jnp.dot(heads_out[...], weights[index], preferred_element_type=jnp.float32)
+        return found.astype(jnp.bfloat16).reshape(2, strip, width)
 
     def add_pair(index):
         pair_copy(index).wait_recv()
@@ -423,70 +451,104 @@
         ).astype(jnp.bfloat16)
         cross_copy(index).start()
 
-    def first(index, carry):
-        pltpu.make_async_copy(weights.at[index], weights.at[index], weight_sems.at[index]).wait()
-        cross_part[index] = partial(1 - chip, index)
-        pair_copy(index).start()
-
-        @pl.when(index > 0)
+    def first(block, carry):
+        attend_strip(1 - chip, block)
+
+        @pl.when(block == 0)
         def _():
-            add_pair(index - 1)
-
+            for load in loads:
+                load.wait()
+
+        def one_chunk(chunk, inner):
+            index = block * chunks + chunk
+            cross_part[index] = partial(chunk)
+            pair_copy(index).start()
+
+            @pl.when(chunk > 0)
+            def _():
+                add_pair(index - 1)
+
+            return inner
+
+        lax.fori_loop(0, chunks, one_chunk, 0)
+        add_pair(block * chunks + chunks - 1)
         return carry
 
-    lax.fori_loop(0, chunks, first, 0)
-    add_pair(chunks - 1)
-
-    def second(index, carry):
-        own_part[index] = partial(chip, index)
-        own_copy(index).start()
+    lax.fori_loop(0, strips, first, 0)
+
+    def second(block, carry):
+        attend_strip(chip, block)
+
+        def one_chunk(chunk, inner):
+            index = block * chunks + chunk
+            own_part[index] = partial(chunk)
+            own_copy(index).start()
+            return inner
+
+        lax.fori_loop(0, chunks, one_chunk, 0)
         return carry
 
-    lax.fori_loop(0, chunks, second, 0)
-
-    def last(index, carry):
+    lax.fori_loop(0, strips, second, 0)
+
+    for index in range(strips * chunks):
         own_copy(index).wait()
         pair_copy(index).wait_send()
         cross_copy(index).wait()
         total = own_part[index, core].astype(jnp.float32) + own_in[index].astype(jnp.float32)
         total = total + cross_in[index].astype(jnp.float32)
-        out_ref[:, pl.ds(pl.multiple_of(index * width, width), width)] = total.astype(jnp.bfloat16)
-        return carry
-
-    lax.fori_loop(0, chunks, last, 0)
-
-
-def combine(heads_out, w_out):
+        block, chunk = index // chunks, index % chunks
+        out_ref[block * strip : (block + 1) * strip, chunk * width : (chunk + 1) * width] = (
+            total.astype(jnp.bfloat16)
+        )
+
+
+def combine(span_order, query, kv, w_out):
     depth, columns = w_out.shape
-    rows = heads_out.shape[0] // 4
+    rows = query.shape[2]
+    ranks = span_order.shape[0]
+    dim = kv.shape[1] // 2
+    strip = rows // STRIPS
     width = columns // CHUNKS
+    sets = 2
+    stacked = depth // dim // sets * 2 * strip
     dma = pltpu.SemaphoreType.DMA
     bf16 = jnp.bfloat16
-    single = pltpu.VMEM((CHUNKS, rows, width), bf16)
-    double = pltpu.VMEM((CHUNKS, 2, rows, width), bf16)
+    steps = STRIPS * CHUNKS
+    single = pltpu.VMEM((steps, strip, width), bf16)
+    double = pltpu.VMEM((steps, 2, strip, width), bf16)
+    state = pltpu.VMEM((sets, stacked, dim), jnp.float32)
     return pl.pallas_call(
-        combine_kernel,
+        functools.partial(combine_kernel, ranks),
         out_shape=jax.ShapeDtypeStruct((rows, columns), bf16),
-        in_specs=[pl.BlockSpec(memory_space=pltpu.VMEM), pl.BlockSpec(memory_space=pl.ANY)],
+        in_specs=[pl.BlockSpec(memory_space=pltpu.SMEM)]
+        + [pl.BlockSpec(memory_space=pltpu.VMEM)]
+        + [pl.BlockSpec(memory_space=pl.ANY)] * 2,
         out_specs=pl.BlockSpec(memory_space=pltpu.VMEM),
         scratch_shapes=[
+            pltpu.VMEM(kv.shape, bf16),
             pltpu.VMEM((CHUNKS, depth, width), bf16),
+            pltpu.VMEM((sets, stacked, dim), bf16),
+            state,
+            state,
+            state,
+            pltpu.VMEM((2 * strip, depth), bf16),
             double,
             single,
             single,
             single,
             double,
             single,
+            dma,
             dma((CHUNKS,)),
-            dma((2, CHUNKS)),
-            dma((2, CHUNKS)),
-            dma((2, CHUNKS)),
+            dma((2, steps)),
+            dma((2, steps)),
+            dma((2, steps)),
         ],
         compiler_params=pltpu.CompilerParams(
-            collective_id=1, has_side_effects=True, vmem_limit_bytes=48 * 2**20
+            collective_id=1, has_side_effects=True, vmem_limit_bytes=60 * 2**20
         ),
         name="combine",
-    )(heads_out.reshape(2, 2, rows, depth), w_out)
+    )(span_order.reshape(-1), query, kv, w_out)
 
 
 def body(tokens, w_query, key_matrix, value_matrix, w_out, span_order):
@@ -507,10 +569,7 @@
     cosine = jnp.concatenate([cosine, cosine], axis=1).reshape(2, 2, rows, dim)
     sine = jnp.concatenate([-sine, sine], axis=1).reshape(2, 2, rows, dim)
     query, kv = project(tokens, w_query, key_matrix, value_matrix, cosine, sine)
-    heads_out = attend(
-        span_order, rank, query.reshape(4 * rows, -1), kv.reshape(-1, 2 * dim)
-    )
-    return combine(heads_out, w_out)
+    return combine(span_order, query, kv.reshape(-1, 2 * dim), w_out)
 
 
 def solution(mesh):

time: 118 us -> 131 us (1.11)
  Pallas kernels: 109 us -> 124 us
  local copies, waits for them, and re-layouts: 7.36 us -> 4.12 us
  other arithmetic: 1.48 us -> 2.97 us
    pallas_call x2 -> x1, Pallas kernels: 56.5 us -> 69.4 us  [combine(): pl.pallas_call(functools.partial(combine_kernel, ranks), out_shape=jax.Sh...]
    unnamed x10 -> x2, local copies, waits for them, and re-layouts: 6.3 us -> 3.45 us
    pallas_call x1, Pallas kernels: 52.1 us -> 54.2 us  [project(): pl.pallas_call(functools.partial(project_kernel, wide, ranks), out_shape=...]
where the time goes in v3:
time: 131 us
  Pallas kernels  124 us (95%)
  local copies, waits for them, and re-layouts  4.12 us (3%)
  other arithmetic  2.97 us (2%)
    pallas_call x1, Pallas kernels, combine(): pl.pallas_call(functools.partial(combine_kernel, ranks), out_shape=jax.Sh...  69.4 us
    pallas_call x1, Pallas kernels, project(): pl.pallas_call(functools.partial(project_kernel, wide, ranks), out_shape=...  54.2 us
    unnamed x2, local copies, waits for them, and re-layouts  3.45 us

profile of v3, /device:TPU:0, one launch (start us, length us, event | category | flops | bytes accessed | tf_op | source)
XLA Modules:
  0.0 130.7 jit_solution(8812313901017963360)
XLA Ops:
  0.0 0.9 multiply_reduce_fusion
  0.9 0.1 add_convert_fusion
  0.9 0.8 copy.8
  1.7 0.7 reshape.83.spans_ref
  2.4 1.0 fusion
  3.4 1.0 pad_maximum_fusion
  4.4 54.2 %project.1 = (bf16[2,2,128,768]{3,2,1,0:T(8,128)(2,1)}, bf16[8,2,2,128,256]{4,3,2,1,0:T(8,128)(2,1)}) custom-call(bf16[128,6144]{1,0:T(8,128)(2,1)} %tokens_ref.1, bf16[6144,768]{1,0:T(8,128)(2,1)} %w_query_ref.1, bf16[6144,128]{1,0:T(8,128)(2,1)} %key_matrix_ref.1, bf16[6144,128]{1,0:T(8,128)(2,1)} %value_matrix_ref.1, ...), custom_call_target="tpu_custom_call" | custom-call | tf_op jit(solution)/shard_map/project/pallas_call | solution.py:257
  58.6 69.4 %combine.1 = bf16[128,6144]{1,0:T(8,128)(2,1)} custom-call(s32[16]{0:T(128)} %reshape.83.spans_ref, bf16[2,2,128,768]{3,2,1,0:T(8,128)(2,1)} %get-tuple-element.7.query_ref, bf16[4096,256]{1,0:T(8,128)(2,1)} %bitcast.1, bf16[768,6144]{1,0:T(8,128)(2,1)} %w_ref.1), custom_call_target="tpu_custom_call" | custom-call | tf_op jit(solution)/shard_map/combine/pallas_call | solution.py:520
  128.0 2.7 %copy.10 = bf16[128,6144]{1,0:T(8,128)(2,1)} copy(bf16[128,6144]{1,0:T(8,128)(2,1)} %combine.1) | data formatting | bytes 3145728
  (1 shorter events, 0.0 us)

commit v4 on v3

--- a/solution.py
+++ b/solution.py
@@ -101,8 +101,8 @@
             (part,),
             across,
         )
-        copy.start()
         far_copies.append(copy)
+    far_copies[0].start()
     near_copy = remote(tokens_ref, near.at[core], near_sems, (), partner)
     near_copy.start()
     own_copy = pltpu.make_async_copy(tokens_ref, near.at[core], local_sems.at[0])
@@ -194,6 +194,7 @@
         staged[...] = kept.reshape(staged.shape)
         share(part, staged)
         if part == 0:
+            far_copies[1].start()
             for load in loads[2:]:
                 load.wait()
 
@@ -217,15 +218,15 @@
         load.wait()
     work(0, near, kv_near)
     for part in range(count):
-        far_copies[part].wait_recv()
+        far_copies[part].wait()
+        if part + 2 < count:
+            far_copies[part + 2].start()
         swap = remote(far.at[part, core], far.at[part, core], swap_sems, (part,), partner)
         swap.start()
         pass_on(part)
         swap.wait()
         work(part + 1, far.at[part], kv_far.at[part])
     pass_on(count)
-    for copy in far_copies:
-        copy.wait_send()
     for part in range(count + 1):
         for step in range(tall):
             for side in range(1, wide):
@@ -331,10 +332,10 @@
         )
         for index in range(chunks)
     ]
+    greet([partner, across])
+    kv_load.wait()
     for load in loads:
         load.start()
-    greet([partner, across])
-    kv_load.wait()
 
     def remote(source, target, sems, index, device):
         return pltpu.make_async_remote_copy(
@@ -424,15 +425,18 @@
             + start
         )
         keep = lax.broadcasted_iota(jnp.int32, shape, 3) <= token
-        tiles([(2 * rank + half, 0.0), entry(2 * lax.rem(rank + 1 - half, ranks))], keep.reshape(stacked, span))
+        def slot(index, at, side):
+            apart = half * (2 * index + at // 2) + (1 - half) * (4 * index + at)
+            return 2 * lax.rem(rank + apart, ranks) + half * side
+
+        others = [entry(slot(0, at, side)) for at, side in ((1, 0), (2, 0), (3, 1))]
+        tiles([(2 * rank + half, 0.0)] + others, keep.reshape(stacked, span))
 
         def step(index, carry):
-            block = lax.rem(rank + half * (1 + index) + (1 - half) * (2 + 2 * index), ranks)
-            later = half + (1 - half) * 2 * lax.rem(rank + 3 + 2 * index, ranks)
-            tiles([entry(2 * block), entry(half * 2 * block + later)], None)
+            tiles([entry(slot(index, at, at % 2)) for at in range(4)], None)
             return carry
 
-        lax.fori_loop(0, (ranks - 2 + ranks * half) // 2, step, 0)
+        lax.fori_loop(1, ranks * (1 + half) // 4, step, 0)
         for one in range(sets):
             total = jnp.sum(totals[one], axis=1, keepdims=True)
             mixed = (accums[one] / total).astype(jnp.bfloat16)
@@ -545,7 +549,7 @@
             dma((2, steps)),
         ],
         compiler_params=pltpu.CompilerParams(
-            collective_id=1, has_side_effects=True, vmem_limit_bytes=60 * 2**20
+            collective_id=1, has_side_effects=True, vmem_limit_bytes=48 * 2**20
         ),
         name="combine",
     )(span_order.reshape(-1), query, kv, w_out)

time: 131 us -> 114 us (0.87)
  Pallas kernels: 124 us -> 106 us
    pallas_call x1, Pallas kernels: 69.4 us -> 51.4 us  [combine(): pl.pallas_call(functools.partial(combine_kernel, ranks), out_shape=jax.Sh...]
    unnamed x2 -> x6, local copies, waits for them, and re-layouts: 3.45 us -> 4.62 us
where the time goes in v4:
time: 114 us; the launch traced here: 113 us
  Pallas kernels  106 us (93%)
  local copies, waits for them, and re-layouts  4.7 us (4%)
  other arithmetic  2.96 us (3%)
    pallas_call x1, Pallas kernels, project(): pl.pallas_call(functools.partial(project_kernel, wide, ranks), out_shape=...  54.2 us
    pallas_call x1, Pallas kernels, combine(): pl.pallas_call(functools.partial(combine_kernel, ranks), out_shape=jax.Sh...  51.4 us
    unnamed x6, local copies, waits for them, and re-layouts  4.62 us

profile of v4, /device:TPU:0, one launch (start us, length us, event | category | flops | bytes accessed | tf_op | source)
XLA Modules:
  0.0 113.3 jit_solution(3703447778274887958)
XLA Ops:
  0.0 0.9 multiply_reduce_fusion
  0.9 0.1 add_convert_fusion
  0.9 0.8 copy.8
  1.7 0.1 reshape.83.spans_ref
  1.8 1.0 fusion
  2.8 1.0 pad_maximum_fusion
  3.8 54.2 %project.1 = (bf16[2,2,128,768]{3,2,1,0:T(8,128)(2,1)}, bf16[8,2,2,128,256]{4,3,2,1,0:T(8,128)(2,1)}) custom-call(bf16[128,6144]{1,0:T(8,128)(2,1)} %tokens_ref.1, bf16[6144,768]{1,0:T(8,128)(2,1)} %w_query_ref.1, bf16[6144,128]{1,0:T(8,128)(2,1)} %key_matrix_ref.1, bf16[6144,128]{1,0:T(8,128)(2,1)} %value_matrix_ref.1, ...), custom_call_target="tpu_custom_call" | custom-call | tf_op jit(solution)/shard_map/project/pallas_call | solution.py:258
  58.0 0.0 copy-start
  58.0 1.6 %copy-done = bf16[8,2,2,128,256]{4,3,2,1,0:T(8,128)(2,1)S(1)} copy-done((bf16[8,2,2,128,256]{4,3,2,1,0:T(8,128)(2,1)S(1)}, bf16[8,2,2,128,256]{4,3,2,1,0:T(8,128)(2,1)}, u32[]{:S(2)}) %copy-start) | copy-done | bytes 2097176
  59.6 0.0 copy-start.1
  59.6 1.1 copy-done.1
  60.7 51.4 %combine.1 = bf16[128,6144]{1,0:T(8,128)(2,1)S(1)} custom-call(s32[16]{0:T(128)S(1)} %reshape.83.spans_ref, bf16[2,2,128,768]{3,2,1,0:T(8,128)(2,1)S(1)} %copy-done.1, bf16[4096,256]{1,0:T(8,128)(2,1)S(1)} %bitcast.1, bf16[768,6144]{1,0:T(8,128)(2,1)} %w_ref.1), custom_call_target="tpu_custom_call" | custom-call | tf_op jit(solution)/shard_map/combine/pallas_call | solution.py:524
  112.2 1.1 %copy.10 = bf16[128,6144]{1,0:T(8,128)(2,1)} copy(bf16[128,6144]{1,0:T(8,128)(2,1)S(1)} %combine.1) | data formatting | bytes 3145728
  (1 shorter events, 0.0 us)
Async XLA Ops:
  58.0 1.6 %copy-start = (bf16[8,2,2,128,256]{4,3,2,1,0:T(8,128)(2,1)S(1)}, bf16[8,2,2,128,256]{4,3,2,1,0:T(8,128)(2,1)}, u32[]{:S(2)}) copy-start(bf16[8,2,2,128,256]{4,3,2,1,0:T(8,128)(2,1)} %get-tuple-element.8) | copy-start | bytes 6291460
  59.6 1.1 %copy-start.1 = (bf16[2,2,128,768]{3,2,1,0:T(8,128)(2,1)S(1)}, bf16[2,2,128,768]{3,2,1,0:T(8,128)(2,1)}, u32[]{:S(2)}) copy-start(bf16[2,2,128,768]{3,2,1,0:T(8,128)(2,1)} %get-tuple-element.7.query_ref) | copy-start | bytes 2359300

commit v5 on v4

--- a/solution.py
+++ b/solution.py
@@ -16,7 +16,7 @@
 
 MESH = pl.DeviceIdType.MESH
 PIECES = 4
-STRIPS = 4
+STRIPS = 2
 CHUNKS = 4
 
 
@@ -133,9 +133,9 @@
 
     def tables(part):
         if part == 0:
-            return cosine_ref[chip], sine_ref[chip]
+            return flat(cosine_ref[chip]), flat(sine_ref[chip])
         span = slice((part - 1) * piece, part * piece)
-        return cosine_ref[1 - chip, :, span], sine_ref[1 - chip, :, span]
+        return flat(cosine_ref[1 - chip, :, span]), flat(sine_ref[1 - chip, :, span])
 
     def flat(values):
         return values.reshape(values.shape[0] * values.shape[1], values.shape[2])
@@ -187,36 +187,44 @@
 
     def work(part, held, staged):
         cosine, sine = tables(part)
-        cosine, sine = flat(cosine), flat(sine)
         both = jnp.dot(flat(held[...]), weights[blocks], preferred_element_type=jnp.float32)
         key = rotate(both[:, :dim], cosine, sine)
         kept = jnp.concatenate([key, both[:, dim:]], axis=1).astype(jnp.bfloat16)
         staged[...] = kept.reshape(staged.shape)
         share(part, staged)
-        if part == 0:
-            far_copies[1].start()
-            for load in loads[2:]:
-                load.wait()
-
-        def one_block(index, carry):
-            found = jnp.dot(flat(held[...]), weights[index], preferred_element_type=jnp.float32)
+
+    def ask_near(index, carry):
+        found = jnp.dot(flat(near[...]), weights[index], preferred_element_type=jnp.float32)
+        cosine, sine = tables(0)
+        for head in range(block // dim):
+            turned = rotate(found[:, head * dim : (head + 1) * dim], cosine, sine)
+            lanes = pl.ds(pl.multiple_of(index * block + head * dim, dim), dim)
+            query_ref[chip, :, :, lanes] = turned.astype(jnp.bfloat16).reshape(2, rows, dim)
+        return carry
+
+    def ask_far(index, carry):
+        held = far[...].reshape(count * 2 * piece, width)
+        found = jnp.dot(held, weights[index], preferred_element_type=jnp.float32)
+        for part in range(count):
+            cosine, sine = tables(part + 1)
             for head in range(block // dim):
-                turned = rotate(found[:, head * dim : (head + 1) * dim], cosine, sine)
-                turned = turned.astype(jnp.bfloat16).reshape(2, -1, dim)
+                one = found[2 * part * piece : 2 * (part + 1) * piece]
+                turned = rotate(one[:, head * dim : (head + 1) * dim], cosine, sine)
                 lanes = pl.ds(pl.multiple_of(index * block + head * dim, dim), dim)
-                if part == 0:
-                    query_ref[chip, :, :, lanes] = turned
-                else:
-                    query_ref[1 - chip, :, (part - 1) * piece : part * piece, lanes] = turned
-            return carry
-
-        lax.fori_loop(0, blocks, one_block, 0)
+                query_ref[1 - chip, :, part * piece : (part + 1) * piece, lanes] = turned.astype(
+                    jnp.bfloat16
+                ).reshape(2, piece, dim)
+        return carry
 
     own_copy.wait()
     near_copy.wait()
     for load in loads[:2]:
         load.wait()
     work(0, near, kv_near)
+    far_copies[1].start()
+    for load in loads[2:]:
+        load.wait()
+    lax.fori_loop(0, blocks, ask_near, 0)
     for part in range(count):
         far_copies[part].wait()
         if part + 2 < count:
@@ -226,7 +234,9 @@
         pass_on(part)
         swap.wait()
         work(part + 1, far.at[part], kv_far.at[part])
+    lax.fori_loop(0, blocks - 1, ask_far, 0)
     pass_on(count)
+    ask_far(blocks - 1, 0)
     for part in range(count + 1):
         for step in range(tall):
             for side in range(1, wide):
@@ -513,7 +523,7 @@
     dim = kv.shape[1] // 2
     strip = rows // STRIPS
     width = columns // CHUNKS
-    sets = 2
+    sets = 3
     stacked = depth // dim // sets * 2 * strip
     dma = pltpu.SemaphoreType.DMA
     bf16 = jnp.bfloat16
@@ -549,7 +559,7 @@
             dma((2, steps)),
         ],
         compiler_params=pltpu.CompilerParams(
-            collective_id=1, has_side_effects=True, vmem_limit_bytes=48 * 2**20
+            collective_id=1, has_side_effects=True, vmem_limit_bytes=60 * 2**20
         ),
         name="combine",
     )(span_order.reshape(-1), query, kv, w_out)

time: 114 us -> 108 us (0.947)
  Pallas kernels: 106 us -> 101 us
    pallas_call x1, Pallas kernels: 51.4 us -> 46.5 us  [combine(): pl.pallas_call(functools.partial(combine_kernel, ranks), out_shape=jax.Sh...]
    unnamed x6 -> x2, local copies, waits for them, and re-layouts: 4.62 us -> 3.45 us
where the time goes in v5:
time: 108 us
  Pallas kernels  101 us (94%)
  local copies, waits for them, and re-layouts  4.12 us (4%)
  other arithmetic  2.97 us (3%)
    pallas_call x1, Pallas kernels, project(): pl.pallas_call(functools.partial(project_kernel, wide, ranks), out_shape=...  54.6 us
    pallas_call x1, Pallas kernels, combine(): pl.pallas_call(functools.partial(combine_kernel, ranks), out_shape=jax.Sh...  46.5 us
    unnamed x2, local copies, waits for them, and re-layouts  3.45 us

profile of v5, /device:TPU:0, one launch (start us, length us, event | category | flops | bytes accessed | tf_op | source)
XLA Modules:
  0.0 108.2 jit_solution(18093917030537164637)
XLA Ops:
  0.0 0.9 multiply_reduce_fusion
  0.9 0.1 add_convert_fusion
  0.9 0.8 copy.8
  1.7 0.7 reshape.83.spans_ref
  2.4 1.0 fusion
  3.4 1.0 pad_maximum_fusion
  4.4 54.6 %project.1 = (bf16[2,2,128,768]{3,2,1,0:T(8,128)(2,1)}, bf16[8,2,2,128,256]{4,3,2,1,0:T(8,128)(2,1)}) custom-call(bf16[128,6144]{1,0:T(8,128)(2,1)} %tokens_ref.1, bf16[6144,768]{1,0:T(8,128)(2,1)} %w_query_ref.1, bf16[6144,128]{1,0:T(8,128)(2,1)} %key_matrix_ref.1, bf16[6144,128]{1,0:T(8,128)(2,1)} %value_matrix_ref.1, ...), custom_call_target="tpu_custom_call" | custom-call | tf_op jit(solution)/shard_map/project/pallas_call | solution.py:268
  59.0 46.5 %combine.1 = bf16[128,6144]{1,0:T(8,128)(2,1)} custom-call(s32[16]{0:T(128)} %reshape.83.spans_ref, bf16[2,2,128,768]{3,2,1,0:T(8,128)(2,1)} %get-tuple-element.7.query_ref, bf16[4096,256]{1,0:T(8,128)(2,1)} %bitcast.1, bf16[768,6144]{1,0:T(8,128)(2,1)} %w_ref.1), custom_call_target="tpu_custom_call" | custom-call | tf_op jit(solution)/shard_map/combine/pallas_call | solution.py:534
  105.5 2.7 %copy.10 = bf16[128,6144]{1,0:T(8,128)(2,1)} copy(bf16[128,6144]{1,0:T(8,128)(2,1)} %combine.1) | data formatting | bytes 3145728
  (1 shorter events, 0.0 us)

commit v6 on v5

--- a/solution.py
+++ b/solution.py
@@ -15,7 +15,7 @@
 
 
 MESH = pl.DeviceIdType.MESH
-PIECES = 4
+PIECES = 8
 STRIPS = 2
 CHUNKS = 4
 
@@ -103,6 +103,7 @@
         )
         far_copies.append(copy)
     far_copies[0].start()
+    far_copies[1].start()
     near_copy = remote(tokens_ref, near.at[core], near_sems, (), partner)
     near_copy.start()
     own_copy = pltpu.make_async_copy(tokens_ref, near.at[core], local_sems.at[0])
@@ -221,22 +222,22 @@
     for load in loads[:2]:
         load.wait()
     work(0, near, kv_near)
-    far_copies[1].start()
+    far_copies[2].start()
     for load in loads[2:]:
         load.wait()
     lax.fori_loop(0, blocks, ask_near, 0)
     for part in range(count):
         far_copies[part].wait()
-        if part + 2 < count:
-            far_copies[part + 2].start()
+        if part + 3 < count:
+            far_copies[part + 3].start()
         swap = remote(far.at[part, core], far.at[part, core], swap_sems, (part,), partner)
         swap.start()
         pass_on(part)
         swap.wait()
         work(part + 1, far.at[part], kv_far.at[part])
-    lax.fori_loop(0, blocks - 1, ask_far, 0)
+    ask_far(0, 0)
     pass_on(count)
-    ask_far(blocks - 1, 0)
+    lax.fori_loop(1, blocks, ask_far, 0)
     for part in range(count + 1):
         for step in range(tall):
             for side in range(1, wide):

time: 108 us -> 123 us (1.14)
  Pallas kernels: 101 us -> 115 us
    pallas_call x1, Pallas kernels: 54.6 us -> 68.9 us  [project(): pl.pallas_call(functools.partial(project_kernel, wide, ranks), out_shape=...]
where the time goes in v6:
time: 123 us; the launch traced here: 122 us
  Pallas kernels  115 us (93%)
  local copies, waits for them, and re-layouts  4.12 us (3%)
  other arithmetic  2.97 us (2%)
    pallas_call x1, Pallas kernels, project(): pl.pallas_call(functools.partial(project_kernel, wide, ranks), out_shape=...  68.9 us
    pallas_call x1, Pallas kernels, combine(): pl.pallas_call(functools.partial(combine_kernel, ranks), out_shape=jax.Sh...  46.5 us
    unnamed x2, local copies, waits for them, and re-layouts  3.45 us

profile of v6, /device:TPU:0, one launch (start us, length us, event | category | flops | bytes accessed | tf_op | source)
XLA Modules:
  0.0 122.5 jit_solution(6905510987993587376)
XLA Ops:
  0.0 0.9 multiply_reduce_fusion
  0.9 0.1 add_convert_fusion
  0.9 0.8 copy.8
  1.7 0.7 reshape.83.spans_ref
  2.4 1.0 fusion
  3.4 1.0 pad_maximum_fusion
  4.4 68.9 %project.1 = (bf16[2,2,128,768]{3,2,1,0:T(8,128)(2,1)}, bf16[8,2,2,128,256]{4,3,2,1,0:T(8,128)(2,1)}) custom-call(bf16[128,6144]{1,0:T(8,128)(2,1)} %tokens_ref.1, bf16[6144,768]{1,0:T(8,128)(2,1)} %w_query_ref.1, bf16[6144,128]{1,0:T(8,128)(2,1)} %key_matrix_ref.1, bf16[6144,128]{1,0:T(8,128)(2,1)} %value_matrix_ref.1, ...), custom_call_target="tpu_custom_call" | custom-call | tf_op jit(solution)/shard_map/project/pallas_call | solution.py:269
  73.3 46.5 %combine.1 = bf16[128,6144]{1,0:T(8,128)(2,1)} custom-call(s32[16]{0:T(128)} %reshape.83.spans_ref, bf16[2,2,128,768]{3,2,1,0:T(8,128)(2,1)} %get-tuple-element.7.query_ref, bf16[4096,256]{1,0:T(8,128)(2,1)} %bitcast.1, bf16[768,6144]{1,0:T(8,128)(2,1)} %w_ref.1), custom_call_target="tpu_custom_call" | custom-call | tf_op jit(solution)/shard_map/combine/pallas_call | solution.py:535
  119.8 2.7 %copy.10 = bf16[128,6144]{1,0:T(8,128)(2,1)} copy(bf16[128,6144]{1,0:T(8,128)(2,1)} %combine.1) | data formatting | bytes 3145728
  (1 shorter events, 0.0 us)
